TPU v7x, 512 devices: a whole 4x8x8 slice. The times are simulated.
512 devices in a mesh: dp: 8 (over y), seq: 64 (over z, x, core).
Axes of the slice: x: 4, y: 8, z: 8, core: 2. Of those that a mesh axis runs over, the one named last changes fastest.
Arguments:
- tokens: bfloat16 [8, 32768, 1024], P('dp', 'seq'), may hold values from -50 to 50
- w_query: bfloat16 [1024, 1024], P(None, 'dp'), may hold values from -0.1875 to 0.1875
- w_key: bfloat16 [1024, 1024], P(None, 'dp'), may hold values from -0.1875 to 0.1875
- w_value: bfloat16 [1024, 1024], P(None, 'dp'), may hold values from -0.1875 to 0.1875
- w_out: bfloat16 [1024, 1024], P('dp'), may hold values from -0.1875 to 0.1875
- norm_gain: float32 [1024], replicated, may hold values from 0.1 to 1.9
Outputs:
- layer_out: bfloat16 [8, 32768, 1024], P('dp', 'seq')
All inputs are finite; a program needn't handle non-finite values.
Results may differ from a plain program's by a relative error of at most 0.017.
Values may be sent and summed in bfloat16 or wider, within the bound.
No kernel may reach another device: no remote copies, remote signals or barrier semaphores. Data moves between devices by JAX's collectives and lax.ppermute only.
A program may use at most 128 MiB of HBM per device.

v0:
```python
import jax
import jax.numpy as jnp
from jax import lax
from jax.sharding import PartitionSpec as P

H = 8
DH = 128


def entering(value, axis, join, neutral):
    place = lax.axis_index(axis)
    gathered = lax.all_gather(value.astype(jnp.bfloat16), axis)
    state = jnp.zeros_like(value) + jnp.asarray(neutral, value.dtype)

    def one(lap, state):
        return join(state, lax.dynamic_index_in_dim(gathered, lap, 0, False).astype(value.dtype))

    return lax.fori_loop(0, place, one, state)


def inner_block(query_heads, key_heads, value_heads):
    length = query_heads.shape[1]
    block = min(length, 512)
    scores = jnp.einsum("hid,hjd->hij", query_heads, key_heads, preferred_element_type=jnp.float32)
    row_ids = jnp.arange(0, block)[:, None]
    col_ids = jnp.arange(block)[None, :]
    scores = jnp.where(col_ids <= row_ids, scores, 0.0).astype(jnp.bfloat16)
    pieces = jnp.einsum("hij,hje->hie", scores, value_heads, preferred_element_type=jnp.float32)
    return pieces


def add_states(earlier, later):
    return earlier + later


def key_value_state(key_heads, value_heads):
    return jnp.einsum("htd,hte->hde", key_heads, value_heads, preferred_element_type=jnp.float32)


def attend(query_heads, key_heads, value_heads, prior):
    within = inner_block(query_heads, key_heads, value_heads)
    carried = jnp.einsum(
        "htd,hde->hte", query_heads, prior.astype(jnp.bfloat16), preferred_element_type=jnp.float32
    )
    return within + carried


def body(tokens, w_query, w_key, w_value, w_out, norm_gain):
    rows = tokens[0]
    length = rows.shape[0]
    full_query, full_key, full_value = (
        lax.all_gather(w_query, "dp", axis=1, tiled=True),
        lax.all_gather(w_key, "dp", axis=1, tiled=True),
        lax.all_gather(w_value, "dp", axis=1, tiled=True),
    )
    query = jnp.dot(rows, full_query, preferred_element_type=jnp.float32).astype(jnp.bfloat16)
    key = jnp.dot(rows, full_key, preferred_element_type=jnp.float32).astype(jnp.bfloat16)
    value = jnp.dot(rows, full_value, preferred_element_type=jnp.float32).astype(jnp.bfloat16)
    query_heads = query.reshape(length, H, DH).transpose(1, 0, 2)
    key_heads = key.reshape(length, H, DH).transpose(1, 0, 2)
    value_heads = value.reshape(length, H, DH).transpose(1, 0, 2)
    local_state = key_value_state(key_heads, value_heads)
    empty_state = jnp.zeros((H, DH, DH), jnp.float32)
    prior = entering(local_state, "seq", add_states, empty_state)
    mixed_raw = attend(query_heads, key_heads, value_heads, prior)
    scale = lax.rsqrt(jnp.mean(mixed_raw * mixed_raw, axis=-1, keepdims=True) + 1e-05)
    normed = (mixed_raw * scale * norm_gain.reshape(H, 1, DH)).astype(jnp.bfloat16)
    normed = normed.transpose(1, 0, 2).reshape(length, H * DH)
    result = jnp.dot(
        normed, lax.all_gather(w_out, "dp", axis=0, tiled=True), preferred_element_type=jnp.float32
    )
    return result.astype(jnp.bfloat16)[None]


def solution(mesh):
    in_specs = (
        P("dp", "seq", None),
        P(None, "dp"),
        P(None, "dp"),
        P(None, "dp"),
        P("dp", None),
        P(),
    )
    out_specs = P("dp", "seq", None)
    return jax.shard_map(body, mesh=mesh, in_specs=in_specs, out_specs=out_specs, check_vma=False)
```

profile of v0, /device:TPU:455, one launch (start us, length us, event | category | flops | bytes accessed | tf_op | source)
XLA Modules:
  0.0 347.7 jit_solution(2035250541791715043)
XLA Ops:
  8.8 46.0 %all-gather.9.cloned.1.call-done = bf16[1024,1024]{1,0:T(8,128)(2,1)} async-done(((bf16[1024,128]{1,0:T(8,128)(2,1)}), bf16[1024,1024]{1,0:T(8,128)(2,1)}) %all-gather.9.cloned.1.call-update) | async-done | bytes 2097168 | tf_op jit(solution)/shard_map/all_gather | solution.py:53
  54.8 2.8 convolution_convert_fusion.2
  58.2 47.8 %all-gather.11.cloned.1.call-done = bf16[1024,1024]{1,0:T(8,128)(2,1)} async-done(((bf16[1024,128]{1,0:T(8,128)(2,1)}), bf16[1024,1024]{1,0:T(8,128)(2,1)}) %all-gather.11.cloned.1.call-update) | async-done | bytes 2097168 | tf_op jit(solution)/shard_map/all_gather | solution.py:54
  106.0 2.8 convolution_convert_fusion.1
  108.8 1.2 convolution_convert_fusion.4
  110.8 1.2 copy.24
  112.0 45.2 %all-gather.7.cloned.1.call-done = bf16[1024,1024]{1,0:T(8,128)(2,1)} async-done(((bf16[1024,128]{1,0:T(8,128)(2,1)}), bf16[1024,1024]{1,0:T(8,128)(2,1)}) %all-gather.7.cloned.1.call-update) | async-done | bytes 2097168 | tf_op jit(solution)/shard_map/all_gather | solution.py:52
  157.2 3.8 %fusion.7 = bf16[64,8,8,128]{3,2,1,0:T(8,128)(2,1)} fusion(bf16[1024,1024]{1,0:T(8,128)(2,1)} %all-gather.7.cloned.1.call-done, bf16[1,512,1024]{2,1,0:T(8,128)(2,1)S(1)} %copy-done), kind=kOutput, calls=%fused_computation.15 | convolution fusion | flops 1074266112 | bytes 4194304 | tf_op jit(solution)/shard_map/dot_general | solution.py:56
  161.0 5.1 %fusion = f32[8,512,128]{1,2,0:T(8,128)} fusion(pred[512,512]{1,0:T(8,128)(4,1)S(1)} %iota_compare_fusion, bf16[8,512,128]{1,2,0:T(8,128)(2,1)S(1)} %bitcast.67, bf16[8,512,128]{2,0,1:T(8,128)(2,1)S(1)} %bitcast.69, bf16[64,8,8,128]{3,2,1,0:T(8,128)(2,1)} %fusion.7), kind=kOutput, calls=%fused_computation.2 | convolution fusion | flops 1077936128 | bytes 5505024 | tf_op jit(solution)/shard_map/hij,hje->hie/dot_general | solution.py:28
  166.1 99.4 %all-gather.15.cloned.1.call-done = bf16[512,128,128]{2,1,0:T(8,128)(2,1)} async-done(((bf16[8,128,128]{2,1,0:T(8,128)(2,1)}), bf16[512,128,128]{2,1,0:T(8,128)(2,1)}) %all-gather.15.cloned.1.call-update) | async-done | bytes 16777232 | tf_op jit(solution)/shard_map/all_gather | solution.py:12
  265.6 69.2 %while.10 = (s32[]{:T(128)}, f32[8,128,128]{2,1,0:T(8,128)S(1)}, s32[]{:T(128)}, bf16[64,8,128,128]{3,2,1,0:T(8,128)(2,1)}, s32[]{:T(128)}, /*index=5*/s32[]{:T(128)}, s32[]{:T(128)}) while((s32[]{:T(128)}, f32[8,128,128]{2,1,0:T(8,128)S(1)}, s32[]{:T(128)}, bf16[64,8,128,128]{3,2,1,0:T(8,128)(2,1)}, s32[]{:T(128)}, /*index=5*/s32[]{:T(128)}, ...), condition=%wide.region_1.2_spmd, body=%wide.region_0.1_spmd.sunk | while | flops 262149 | bytes 1310835 | solution.py:18
  265.6 1.2 convert_add_fusion.2
  266.8 1.1 convert_add_fusion.2
  267.9 1.1 convert_add_fusion.2
  269.0 1.1 convert_add_fusion.2
  270.1 1.1 convert_add_fusion.2
  271.2 1.1 convert_add_fusion.2
  272.3 1.1 convert_add_fusion.2
  273.4 1.1 convert_add_fusion.2
  274.5 1.1 convert_add_fusion.2
  275.6 1.1 convert_add_fusion.2
  276.7 1.1 convert_add_fusion.2
  277.8 1.1 convert_add_fusion.2
  278.9 1.1 convert_add_fusion.2
  280.0 1.1 convert_add_fusion.2
  281.1 1.1 convert_add_fusion.2
  282.2 1.1 convert_add_fusion.2
  285.4 1.1 convert_add_fusion.2
  286.5 1.1 convert_add_fusion.2
  287.6 1.1 convert_add_fusion.2
  288.7 1.1 convert_add_fusion.2
  290.9 1.1 convert_add_fusion.2
  292.0 1.1 convert_add_fusion.2
  293.1 1.1 convert_add_fusion.2
  294.2 1.1 convert_add_fusion.2
  295.3 1.1 convert_add_fusion.2
  296.4 1.1 convert_add_fusion.2
  297.5 1.1 convert_add_fusion.2
  298.6 1.1 convert_add_fusion.2
  299.7 1.1 convert_add_fusion.2
  300.8 1.1 convert_add_fusion.2
  301.9 1.1 convert_add_fusion.2
  303.0 1.1 convert_add_fusion.2
  305.2 1.1 convert_add_fusion.2
  306.3 1.1 convert_add_fusion.2
  307.4 1.1 convert_add_fusion.2
  310.7 1.1 convert_add_fusion.2
  311.8 1.1 convert_add_fusion.2
  312.9 1.1 convert_add_fusion.2
  315.1 1.1 convert_add_fusion.2
  316.2 1.1 convert_add_fusion.2
  317.3 1.1 convert_add_fusion.2
  318.4 1.1 convert_add_fusion.2
  320.6 1.1 convert_add_fusion.2
  321.7 1.1 convert_add_fusion.2
  322.8 1.1 convert_add_fusion.2
  326.0 1.1 convert_add_fusion.2
  327.1 1.1 convert_add_fusion.2
  328.2 1.1 convert_add_fusion.2
  331.5 1.1 convert_add_fusion.2
  332.6 1.1 convert_add_fusion.2
  333.7 1.1 convert_add_fusion.2
  334.8 2.1 multiply_reduce_fusion
  337.4 3.8 %fusion.8 = bf16[1,512,1024]{2,1,0:T(8,128)(2,1)} fusion(bf16[512,1024]{0,1:T(8,128)(2,1)S(1)} %bitcast.65, bf16[1024,1024]{1,0:T(8,128)(2,1)} %all-gather.13.cloned.1.call-done), kind=kOutput, calls=%fused_computation.16 | convolution fusion | flops 1074266112 | bytes 4194304 | tf_op jit(solution)/shard_map/dot_general | solution.py:69
  (36 shorter events, 16.7 us)
Async XLA Ops:
  6.5 48.3 %copy-start = (bf16[1,512,1024]{2,1,0:T(8,128)(2,1)S(1)}, bf16[1,512,1024]{2,1,0:T(8,128)(2,1)}, u32[]{:S(2)}) copy-start(bf16[1,512,1024]{2,1,0:T(8,128)(2,1)} %param.8) | copy-start | bytes 3145732
  6.5 48.3 %all-gather.9.cloned.1.call-start = ((), (), s32[]{:S(2)}) async-start(), calls=%async_computation.1 | async-start | bytes 2359296 | tf_op jit(solution)/shard_map/all_gather | solution.py:53
  7.3 98.7 %all-gather.11.cloned.1.call-start = ((), (), s32[]{:S(2)}) async-start(), calls=%async_computation.2 | async-start | bytes 2359296 | tf_op jit(solution)/shard_map/all_gather | solution.py:54
  8.0 149.2 %all-gather.7.cloned.1.call-start = ((), (), s32[]{:S(2)}) async-start(), calls=%async_computation | async-start | bytes 2359296 | tf_op jit(solution)/shard_map/all_gather | solution.py:52
  8.7 256.8 %all-gather.15.cloned.1.call-start = ((), (), s32[]{:S(2)}) async-start(), calls=%async_computation.4 | async-start | bytes 17039360 | tf_op jit(solution)/shard_map/all_gather | solution.py:12
  110.1 227.3 %all-gather.13.cloned.1.call-start = ((), (), s32[]{:S(2)}) async-start(), calls=%async_computation.3 | async-start | bytes 2359296 | tf_op jit(solution)/shard_map/all_gather | solution.py:70
  112.0 49.0 %copy-start.1 = (bf16[64,8,8,128]{3,2,1,0:T(8,128)(2,1)S(1)}, bf16[64,8,8,128]{3,2,1,0:T(8,128)(2,1)}, u32[]{:S(2)}) copy-start(bf16[64,8,8,128]{3,2,1,0:T(8,128)(2,1)} %copy.24) | copy-start | bytes 3145732
  265.6 69.2 %copy-start.2 = (bf16[64,8,8,128]{3,2,1,0:T(8,128)(2,1)S(1)}, bf16[64,8,8,128]{3,2,1,0:T(8,128)(2,1)}, u32[]{:S(2)}) copy-start(bf16[64,8,8,128]{3,2,1,0:T(8,128)(2,1)} %fusion.7) | copy-start | bytes 3145732
  334.8 2.2 copy-start.3
Sparse Core Ops, SparseCore 0:
  9.4 45.3 all-gather.8
  56.8 49.1 all-gather.10
  108.0 49.1 all-gather.6
  160.4 105.0 all-gather.14
  267.5 40.4 all-gather.12
where the time goes:
time: 350 us; the launch traced here: 348 us
  waiting for transfers between devices  241 us (69%)
  other arithmetic  67.9 us (19%)
  matrix products  21.8 us (6%)
  between operations  13.2 us (4%)
    all_gather x1, waiting for transfers between devices, entering(): gathered = lax.all_gather(value.astype(jnp.bfloat16), axis)  99.4 us
    add x63, other arithmetic, add_states(): return earlier + later  67.5 us
    all_gather x1, waiting for transfers between devices, body(): lax.all_gather(w_value, 'dp', axis=1, tiled=True)  47.8 us
    all_gather x1, waiting for transfers between devices, body(): lax.all_gather(w_key, 'dp', axis=1, tiled=True)  46 us
    all_gather x1, waiting for transfers between devices, body(): lax.all_gather(w_query, 'dp', axis=1, tiled=True)  45.2 us
  transfers between devices with their start and end apart: 5, of which 4 were waited for; matrix products, arithmetic and copies ran while one was open for 25% of the time, Pallas kernels for 0%

commit v1 on v0

--- a/solution.py
+++ b/solution.py
@@ -5,6 +5,11 @@
 
 H = 8
 DH = 128
+
+
+def gather_by_exchange(array, axis, dim):
+    copies = jnp.concatenate([array] * lax.axis_size(axis), axis=dim)
+    return lax.all_to_all(copies, axis, dim, dim, tiled=True)
 
 
 def entering(value, axis, join, neutral):
@@ -50,7 +55,7 @@
     length = rows.shape[0]
     full_query, full_key, full_value = (
         lax.all_gather(w_query, "dp", axis=1, tiled=True),
-        lax.all_gather(w_key, "dp", axis=1, tiled=True),
+        gather_by_exchange(w_key, "dp", 1),
         lax.all_gather(w_value, "dp", axis=1, tiled=True),
     )
     query = jnp.dot(rows, full_query, preferred_element_type=jnp.float32).astype(jnp.bfloat16)

time: 350 us -> 331 us (0.946)
  waiting for transfers between devices: 241 us -> 211 us
  starting transfers between devices: 0.16 us -> 6.94 us
  local copies, waits for them, and re-layouts: 1.84 us -> 6.57 us
    all_to_all x0 -> x1, waiting for transfers between devices: none -> 63.6 us  [gather_by_exchange(): return lax.all_to_all(copies, axis, dim, dim, tiled=True)]
    all_gather x1 -> x0, waiting for transfers between devices: 46 us -> none  [body(): lax.all_gather(w_key, 'dp', axis=1, tiled=True)]
    all_gather x1, waiting for transfers between devices: 47.8 us -> 4.98 us  [body(): lax.all_gather(w_value, 'dp', axis=1, tiled=True)]
    all_to_all x0 -> x1, starting transfers between devices: none -> 6.82 us  [gather_by_exchange(): return lax.all_to_all(copies, axis, dim, dim, tiled=True)]
    all_gather x1, waiting for transfers between devices: 45.2 us -> 39.9 us  [body(): lax.all_gather(w_query, 'dp', axis=1, tiled=True)]
    all_to_all x0 -> x2, local copies, waits for them, and re-layouts: none -> 5 us  [gather_by_exchange(): return lax.all_to_all(copies, axis, dim, dim, tiled=True)]
  transfers between devices with their start and end apart: 5 -> 5, of which waited for: 4 -> 4; matrix products, arithmetic and copies ran while one was open for 25% -> 28% of each run, Pallas kernels for 0% -> 0%
where the time goes in v1:
time: 331 us; the launch traced here: 328 us
  waiting for transfers between devices  211 us (64%)
  other arithmetic  67.9 us (21%)
  matrix products  21.2 us (6%)
  between operations  13.3 us (4%)
  starting transfers between devices  6.94 us (2%)
  local copies, waits for them, and re-layouts  6.57 us (2%)
    all_gather x1, waiting for transfers between devices, entering(): gathered = lax.all_gather(value.astype(jnp.bfloat16), axis)  100 us
    add x63, other arithmetic, add_states(): return earlier + later  67.5 us
    all_to_all x1, waiting for transfers between devices, gather_by_exchange(): return lax.all_to_all(copies, axis, dim, dim, tiled=True)  63.6 us
    all_gather x1, waiting for transfers between devices, body(): lax.all_gather(w_query, 'dp', axis=1, tiled=True)  39.9 us
    all_to_all x1, starting transfers between devices, gather_by_exchange(): return lax.all_to_all(copies, axis, dim, dim, tiled=True)  6.82 us
  transfers between devices with their start and end apart: 5, of which 4 were waited for; matrix products, arithmetic and copies ran while one was open for 28% of the time, Pallas kernels for 0%

profile of v1, /device:TPU:455, one launch (start us, length us, event | category | flops | bytes accessed | tf_op | source)
XLA Modules:
  0.0 328.2 jit_solution(16063447791426921677)
XLA Ops:
  7.3 1.1 copy.16
  8.6 2.4 copy.24
  11.0 6.8 %all-to-all-start = ((bf16[1024,8,128]{2,0,1:T(8,128)(2,1)}), bf16[1024,8,128]{2,0,1:T(8,128)(2,1)S(1)}, u32[]{:S(2)}, u32[]{:S(2)}) async-start(bf16[1024,8,128]{2,0,1:T(8,128)(2,1)} %copy.24), calls=%async_computation | async-start | bytes 4194304 | tf_op jit(solution)/shard_map/all_to_all | solution.py:12
  18.6 63.6 %all-to-all-done = bf16[1024,8,128]{2,0,1:T(8,128)(2,1)S(1)} async-done(((bf16[1024,8,128]{2,0,1:T(8,128)(2,1)}), bf16[1024,8,128]{2,0,1:T(8,128)(2,1)S(1)}, u32[]{:S(2)}, u32[]{:S(2)}) %all-to-all-start) | async-done | bytes 2097184 | tf_op jit(solution)/shard_map/all_to_all | solution.py:12
  82.1 2.6 copy.25
  84.7 2.9 convolution_convert_fusion.2
  87.6 5.0 %all-gather.8.cloned.1.call-done = bf16[1024,1024]{1,0:T(8,128)(2,1)} async-done(((bf16[1024,128]{1,0:T(8,128)(2,1)}), bf16[1024,1024]{1,0:T(8,128)(2,1)}) %all-gather.8.cloned.1.call-update) | async-done | bytes 2097168 | tf_op jit(solution)/shard_map/all_gather | solution.py:59
  92.6 2.8 convolution_convert_fusion.1
  95.5 1.2 convolution_convert_fusion.4
  97.6 39.9 %all-gather.6.cloned.1.call-done = bf16[1024,1024]{1,0:T(8,128)(2,1)} async-done(((bf16[1024,128]{1,0:T(8,128)(2,1)}), bf16[1024,1024]{1,0:T(8,128)(2,1)}) %all-gather.6.cloned.1.call-update) | async-done | bytes 2097168 | tf_op jit(solution)/shard_map/all_gather | solution.py:57
  137.6 2.8 fusion.7
  140.4 5.5 %fusion = f32[8,512,128]{1,2,0:T(8,128)} fusion(pred[512,512]{1,0:T(8,128)(4,1)S(1)} %iota_compare_fusion, bf16[8,512,128]{1,2,0:T(8,128)(2,1)} %bitcast.77, bf16[8,512,128]{2,0,1:T(8,128)(2,1)S(1)} %bitcast.73, bf16[64,8,8,128]{3,2,1,0:T(8,128)(2,1)S(1)} %fusion.7), kind=kOutput, calls=%fused_computation.2 | convolution fusion | flops 1077936128 | bytes 5505024 | tf_op jit(solution)/shard_map/hij,hje->hie/dot_general | solution.py:33
  146.0 100.1 %all-gather.12.cloned.1.call-done = bf16[512,128,128]{2,1,0:T(8,128)(2,1)} async-done(((bf16[8,128,128]{2,1,0:T(8,128)(2,1)}), bf16[512,128,128]{2,1,0:T(8,128)(2,1)}) %all-gather.12.cloned.1.call-update) | async-done | bytes 16777232 | tf_op jit(solution)/shard_map/all_gather | solution.py:17
  246.1 69.2 %while.10 = (s32[]{:T(128)}, f32[8,128,128]{2,1,0:T(8,128)S(1)}, s32[]{:T(128)}, bf16[64,8,128,128]{3,2,1,0:T(8,128)(2,1)}, s32[]{:T(128)}, /*index=5*/s32[]{:T(128)}, s32[]{:T(128)}) while((s32[]{:T(128)}, f32[8,128,128]{2,1,0:T(8,128)S(1)}, s32[]{:T(128)}, bf16[64,8,128,128]{3,2,1,0:T(8,128)(2,1)}, s32[]{:T(128)}, /*index=5*/s32[]{:T(128)}, ...), condition=%wide.region_1.2_spmd, body=%wide.region_0.1_spmd.sunk | while | flops 262149 | bytes 1310835 | solution.py:23
  246.2 1.2 convert_add_fusion.2
  247.3 1.1 convert_add_fusion.2
  249.5 1.1 convert_add_fusion.2
  250.6 1.1 convert_add_fusion.2
  251.7 1.1 convert_add_fusion.2
  252.8 1.1 convert_add_fusion.2
  255.0 1.1 convert_add_fusion.2
  256.1 1.1 convert_add_fusion.2
  257.2 1.1 convert_add_fusion.2
  260.5 1.1 convert_add_fusion.2
  261.6 1.1 convert_add_fusion.2
  262.7 1.1 convert_add_fusion.2
  263.8 1.1 convert_add_fusion.2
  264.9 1.1 convert_add_fusion.2
  266.0 1.1 convert_add_fusion.2
  268.2 1.1 convert_add_fusion.2
  269.3 1.1 convert_add_fusion.2
  270.4 1.1 convert_add_fusion.2
  271.5 1.1 convert_add_fusion.2
  272.6 1.1 convert_add_fusion.2
  274.8 1.1 convert_add_fusion.2
  275.9 1.1 convert_add_fusion.2
  277.0 1.1 convert_add_fusion.2
  278.1 1.1 convert_add_fusion.2
  279.2 1.1 convert_add_fusion.2
  280.3 1.1 convert_add_fusion.2
  281.4 1.1 convert_add_fusion.2
  282.5 1.1 convert_add_fusion.2
  283.6 1.1 convert_add_fusion.2
  286.8 1.1 convert_add_fusion.2
  287.9 1.1 convert_add_fusion.2
  289.0 1.1 convert_add_fusion.2
  291.2 1.1 convert_add_fusion.2
  292.3 1.1 convert_add_fusion.2
  293.4 1.1 convert_add_fusion.2
  294.5 1.1 convert_add_fusion.2
  296.7 1.1 convert_add_fusion.2
  297.8 1.1 convert_add_fusion.2
  298.9 1.1 convert_add_fusion.2
  302.2 1.1 convert_add_fusion.2
  303.3 1.1 convert_add_fusion.2
  304.4 1.1 convert_add_fusion.2
  307.7 1.1 convert_add_fusion.2
  308.8 1.1 convert_add_fusion.2
  309.9 1.1 convert_add_fusion.2
  312.1 1.1 convert_add_fusion.2
  313.2 1.1 convert_add_fusion.2
  314.3 1.1 convert_add_fusion.2
  315.4 2.1 multiply_reduce_fusion
  317.9 3.8 %fusion.8 = bf16[1,512,1024]{2,1,0:T(8,128)(2,1)} fusion(bf16[512,1024]{0,1:T(8,128)(2,1)S(1)} %bitcast.69, bf16[1024,1024]{1,0:T(8,128)(2,1)} %all-gather.10.cloned.1.call-done), kind=kOutput, calls=%fused_computation.16 | convolution fusion | flops 1074266112 | bytes 4194304 | tf_op jit(solution)/shard_map/dot_general | solution.py:74
  (47 shorter events, 19.0 us)
Async XLA Ops:
  6.5 78.2 %copy-start = (bf16[1,512,1024]{2,1,0:T(8,128)(2,1)S(1)}, bf16[1,512,1024]{2,1,0:T(8,128)(2,1)}, u32[]{:S(2)}) copy-start(bf16[1,512,1024]{2,1,0:T(8,128)(2,1)} %param.8) | copy-start | bytes 3145732
  6.5 86.1 %all-gather.8.cloned.1.call-start = ((), (), s32[]{:S(2)}) async-start(), calls=%async_computation.2 | async-start | bytes 2359296 | tf_op jit(solution)/shard_map/all_gather | solution.py:59
  11.0 71.2 %all-to-all-start = ((bf16[1024,8,128]{2,0,1:T(8,128)(2,1)}), bf16[1024,8,128]{2,0,1:T(8,128)(2,1)S(1)}, u32[]{:S(2)}, u32[]{:S(2)}) async-start(bf16[1024,8,128]{2,0,1:T(8,128)(2,1)} %copy.24), calls=%async_computation | async-start | bytes 4194304 | tf_op jit(solution)/shard_map/all_to_all | solution.py:12
  17.8 119.8 %all-gather.6.cloned.1.call-start = ((), (), s32[]{:S(2)}) async-start(), calls=%async_computation.1 | async-start | bytes 2359296 | tf_op jit(solution)/shard_map/all_gather | solution.py:57
  18.5 227.5 %all-gather.12.cloned.1.call-start = ((), (), s32[]{:S(2)}) async-start(), calls=%async_computation.4 | async-start | bytes 17039360 | tf_op jit(solution)/shard_map/all_gather | solution.py:17
  87.6 7.8 %copy-start.4 = (bf16[1024,512]{1,0:T(8,128)(2,1)}, bf16[1024,512]{1,0:T(8,128)(2,1)S(1)}, u32[]{:S(2)}) copy-start(bf16[1024,512]{1,0:T(8,128)(2,1)S(1)} %convolution_convert_fusion.2) | copy-start | bytes 3145732
  96.7 221.2 %all-gather.10.cloned.1.call-start = ((), (), s32[]{:S(2)}) async-start(), calls=%async_computation.3 | async-start | bytes 2359296 | tf_op jit(solution)/shard_map/all_gather | solution.py:75
  140.4 5.5 %copy-start.1 = (bf16[64,8,8,128]{3,2,1,0:T(8,128)(2,1)}, bf16[64,8,8,128]{3,2,1,0:T(8,128)(2,1)S(1)}, u32[]{:S(2)}) copy-start(bf16[64,8,8,128]{3,2,1,0:T(8,128)(2,1)S(1)} %fusion.7) | copy-start | bytes 3145732
  246.1 69.2 %copy-start.2 = (bf16[64,8,8,128]{3,2,1,0:T(8,128)(2,1)S(1)}, bf16[64,8,8,128]{3,2,1,0:T(8,128)(2,1)}, u32[]{:S(2)}) copy-start(bf16[64,8,8,128]{3,2,1,0:T(8,128)(2,1)} %copy-done.1) | copy-start | bytes 3145732
  315.3 2.2 copy-start.3
Sparse Core Ops, SparseCore 0:
  9.4 83.2 all-gather.7
  94.6 42.9 all-gather.5
  140.9 105.0 all-gather.11
  248.0 40.4 all-gather.9
